TPU v7x, 32 devices: a whole 2x2x4 slice. The times are simulated.
32 devices in a mesh: row: 8 (over y, x, core), col: 4 (over z).
Axes of the slice: x: 2, y: 2, z: 4, core: 2. Of those that a mesh axis runs over, the one named last changes fastest.
Arguments:
- frames: bfloat16 [4, 4096, 512], P(None, 'row'), may hold values from -6 to 6
- orders: int32 [2, 2], replicated, may hold values from 1 to 64
- owners: int32 [4096, 1], P(('row', 'col')), may hold values from 0 to 31; in each aligned block of 128 rows (0 to 127, 128 to 255, ...) at most 8 rows name the same one
- templates: bfloat16 [32, 512, 128], P(('row', 'col')), may hold values from -0.25 to 0.25
Outputs:
- spectrum: bfloat16 [2, 4, 4, 2048, 4096], P(None, None, None, ('row', 'col'))
- detections: bfloat16 [32, 32, 8, 64, 128], P(('row', 'col'))
Inputs may be any that keep to these rules, and one draw needn't show every extreme that they name: `owners`: rows 128 * i to 128 * (i + 1) - 1 hold the tiles of the device with index i along row+col. At most 8 tiles of one device name the same owner, and some device reaches that in every draw.
All inputs are finite; a program needn't handle non-finite values.
Results may differ from a plain program's by a relative error of at most 0.0078.
Values may be sent and summed in bfloat16 or wider, within the bound.
A program may use at most 192 MiB of HBM per device.

v0:
```python
import functools
import math

import jax
import jax.numpy as jnp
from jax import lax
from jax.experimental import pallas as pl
from jax.experimental.pallas import tpu as pltpu
from jax.sharding import PartitionSpec as P

RADIX = 8
F32 = jnp.float32
BF16 = jnp.bfloat16


def channel_table(n_total, channel_ids):
    position = jnp.arange(n_total, dtype=jnp.int32)
    turns = position[None, :] * channel_ids[:, None] % n_total
    phase_angle = 2.0 * math.pi / n_total * turns.astype(F32)
    window = 0.5 - 0.5 * jnp.cos(2.0 * math.pi / n_total * position.astype(F32))
    weighted = math.sqrt(8.0 / (3.0 * n_total)) * window[None, :]
    both = jnp.concatenate(
        [weighted * jnp.cos(phase_angle), weighted * jnp.sin(phase_angle)], axis=0
    )
    return both.astype(BF16)


def sub_table(sub_total):
    index = jnp.arange(sub_total, dtype=jnp.int32)
    turns = index[:, None] * index[None, :] % sub_total
    phase_angle = 2.0 * math.pi / sub_total * turns.astype(F32)
    cos, sin = jnp.cos(phase_angle).astype(BF16), jnp.sin(phase_angle).astype(BF16)
    return jnp.concatenate(
        [jnp.concatenate([cos, -sin], axis=1), jnp.concatenate([sin, cos], axis=1)], axis=0
    )


def twist_table(sub_total, hops_total):
    index_b = jnp.arange(RADIX, dtype=jnp.int32)[:, None]
    index_p = jnp.arange(sub_total, dtype=jnp.int32)[None, :]
    angle = 2.0 * math.pi / hops_total * (index_b * index_p % hops_total).astype(F32)
    return jnp.concatenate([jnp.cos(angle), jnp.sin(angle)], axis=0) / math.sqrt(hops_total)


def dot_nt(a, b):
    return lax.dot_general(a, b, (((1,), (1,)), ((), ())), preferred_element_type=F32)


def four_point(y0, y1, y2, y3):
    s0 = (y0[0] + y2[0], y0[1] + y2[1])
    s1 = (y0[0] - y2[0], y0[1] - y2[1])
    s2 = (y1[0] + y3[0], y1[1] + y3[1])
    s3 = (y1[0] - y3[0], y1[1] - y3[1])
    return (
        (s0[0] + s2[0], s0[1] + s2[1]),
        (s1[0] + s3[1], s1[1] - s3[0]),
        (s0[0] - s2[0], s0[1] - s2[1]),
        (s1[0] - s3[1], s1[1] + s3[0]),
    )


def eight_point(x):
    even = four_point(x[0], x[2], x[4], x[6])
    odd = four_point(x[1], x[3], x[5], x[7])
    h = math.sqrt(0.5)
    o1, o2, o3 = odd[1], odd[2], odd[3]
    turned = (
        odd[0],
        ((o1[0] + o1[1]) * h, (o1[1] - o1[0]) * h),
        (o2[1], -o2[0]),
        ((o3[1] - o3[0]) * h, -(o3[0] + o3[1]) * h),
    )
    low = [(e[0] + t[0], e[1] + t[1]) for e, t in zip(even, turned)]
    high = [(e[0] - t[0], e[1] - t[1]) for e, t in zip(even, turned)]
    return low + high


def log_one_plus(x):
    return jnp.where(x < 2.0**-8, x * (1.0 - 0.5 * x), jnp.log(1.0 + x))


def spectra_kernel(
    orders_ref, owners_ref, places_ref, first_ref,
    frames_ref, coef_ref, table_ref, twist_ref, templates_ref,
    spectrum_ref, outgoing_ref,
    demod, product, section, feature,
    *, combos, per,
):
    sensor, combo = pl.program_id(0), pl.program_id(1)
    sub = table_ref.shape[0] // 2
    frame = frames_ref.shape[-1]
    wide = 2 * per

    @pl.when((sensor == 0) & (combo == 0))
    def _():
        outgoing_ref[...] = jnp.zeros_like(outgoing_ref)

    @pl.when(combo == 0)
    def _():
        channel = first_ref[0] + lax.broadcasted_iota(jnp.int32, (wide, sub), 0)
        last = lax.broadcasted_iota(jnp.int32, (2 * wide, sub), 1) == sub - 1
        for b in range(RADIX):
            total, ahead = None, None
            for quarter in range(4):
                hops = frames_ref[:, 0, (b + quarter) % RADIX].reshape(sub, frame)
                part = dot_nt(coef_ref[:, quarter * frame : (quarter + 1) * frame], hops)
                if b + quarter < RADIX:
                    total = part if total is None else total + part
                else:
                    ahead = part if ahead is None else ahead + part
            if ahead is not None:
                moved = pltpu.roll(ahead, sub - 1, 1)
                total = total + jnp.where(last, 0.0, moved)
            a_cos, a_sin = total[:wide], total[wide:]
            turn = channel % 4 * (b % 4) % 4
            swap = (turn == 1) | (turn == 3)
            real = jnp.where(swap, a_sin, a_cos)
            imag = jnp.where(swap, a_cos, a_sin)
            real = jnp.where((turn == 1) | (turn == 2), -real, real)
            imag = jnp.where((turn == 0) | (turn == 1), -imag, imag)
            demod[0, b] = real.astype(BF16)
            demod[1, b] = imag.astype(BF16)
        row = lax.broadcasted_iota(jnp.int32, (per, wide), 0)
        col = lax.broadcasted_iota(jnp.int32, (per, wide), 1)
        pick = jnp.concatenate(
            [(col == row + orders_ref[c]).astype(F32) for c in range(combos)], axis=0
        ).astype(BF16)
        for b in range(RADIX):
            part_real = jnp.dot(pick, demod[0, b], preferred_element_type=F32)
            part_imag = jnp.dot(pick, demod[1, b], preferred_element_type=F32)
            own_real = demod[0, b, :per].astype(F32)
            own_imag = demod[1, b, :per].astype(F32)
            for c in range(combos):
                pr = part_real[c * per : (c + 1) * per]
                pi = part_imag[c * per : (c + 1) * per]
                rows = slice(b * per, (b + 1) * per)
                product[c, rows, :sub] = (own_real * pr + own_imag * pi).astype(BF16)
                product[c, rows, sub:] = (own_imag * pr - own_real * pi).astype(BF16)

    section[...] = jnp.dot(product[combo], table_ref[...], preferred_element_type=F32)

    def rows_step(at, carry):
        start = pl.multiple_of(at * 16, 16)
        for lane in range(0, sub, 128):
            values = []
            for b in range(RADIX):
                here = pl.ds(b * per + start, 16)
                re = section[here, lane : lane + 128]
                im = section[here, sub + lane : sub + lane + 128]
                cos = twist_ref[b : b + 1, lane : lane + 128]
                sin = twist_ref[RADIX + b : RADIX + b + 1, lane : lane + 128]
                values.append((re * cos + im * sin, im * cos - re * sin))
            for d, (re, im) in enumerate(eight_point(values)):
                out = slice(d * sub + lane, d * sub + lane + 128)
                spectrum_ref[0, 0, 0, pl.ds(start, 16), out] = re.astype(BF16)
                spectrum_ref[1, 0, 0, pl.ds(start, 16), out] = im.astype(BF16)
                feature[d, pl.ds(start, 16), lane : lane + 128] = log_one_plus(
                    re * re + im * im
                ).astype(BF16)
        return carry

    lax.fori_loop(0, per // 16, rows_step, 0)

    first_tile = (sensor * combos + combo) * RADIX
    for d in range(RADIX):
        owner = owners_ref[first_tile + d]
        place = places_ref[first_tile + d]
        outgoing_ref[place] = jnp.dot(
            feature[d], templates_ref[owner], preferred_element_type=F32
        ).astype(BF16)


def shards(frames, orders, owners, templates):
    rows_count = lax.axis_size("row")
    cols_count = lax.axis_size("col")
    devices_n = rows_count * cols_count
    sensors, hop_dev, frame_len = frames.shape
    channels_n = 4 * frame_len
    hops_n = hop_dev * rows_count
    sub_n = hops_n // RADIX
    per = channels_n // devices_n
    combos = orders.shape[0] * orders.shape[1]
    feat_n = templates.shape[2]
    row_at = lax.axis_index("row")
    col_at = lax.axis_index("col")

    part = sub_n // devices_n
    mine = lax.dynamic_slice_in_dim(
        frames.reshape(sensors, hop_dev // RADIX, RADIX, frame_len), col_at * part, part, axis=1
    ).transpose(0, 2, 1, 3)
    hops = lax.all_gather(mine, ("row", "col"), axis=0)
    if part % 16:
        hops = hops.transpose(1, 2, 0, 3, 4).reshape(1, sensors, RADIX, sub_n, frame_len)
    gathered = lax.all_gather(templates, ("row", "col"), axis=0, tiled=True)

    first_channel = (row_at * cols_count + col_at) * per
    channel_ids = (first_channel + jnp.arange(2 * per, dtype=jnp.int32)) % channels_n
    coefficients = channel_table(channels_n, channel_ids)
    table = sub_table(sub_n)
    twist = twist_table(sub_n, hops_n)

    tiles_dev = sensors * combos * RADIX
    capacity = max(2, 2 * tiles_dev // devices_n)
    owner_ids = owners[:, 0]
    index = jnp.arange(tiles_dev, dtype=jnp.int32)
    earlier = (owner_ids[None, :] == owner_ids[:, None]) & (index[None, :] < index[:, None])
    places = owner_ids * capacity + jnp.sum(earlier.astype(jnp.int32), axis=1)

    whole = lambda shape: pl.BlockSpec(
        shape, lambda s, c, *_: (0,) * len(shape), pipeline_mode=pl.Buffered(1)
    )
    blocks = hops.shape[0]
    flops = 2 * sensors * hops_n * channels_n * 4 * per + 2 * sensors * combos * RADIX * per * 4 * sub_n * sub_n
    spectrum, outgoing = pl.pallas_call(
        functools.partial(spectra_kernel, combos=combos, per=per),
        grid_spec=pltpu.PrefetchScalarGridSpec(
            num_scalar_prefetch=4,
            grid=(sensors, combos),
            in_specs=[
                pl.BlockSpec(
                    (blocks, 1, RADIX, hops.shape[3], frame_len),
                    lambda s, c, *_: (0, s, 0, 0, 0),
                ),
                whole(coefficients.shape),
                whole(table.shape),
                whole(twist.shape),
                whole(gathered.shape),
            ],
            out_specs=[
                pl.BlockSpec((2, 1, 1, per, hops_n), lambda s, c, *_: (0, s, c, 0, 0)),
                whole((devices_n * capacity, per, feat_n)),
            ],
            scratch_shapes=[
                pltpu.VMEM((2, RADIX, 2 * per, sub_n), BF16),
                pltpu.VMEM((combos, RADIX * per, 2 * sub_n), BF16),
                pltpu.VMEM((RADIX * per, 2 * sub_n), F32),
                pltpu.VMEM((RADIX, per, sub_n), BF16),
            ],
        ),
        out_shape=[
            jax.ShapeDtypeStruct((2, sensors, combos, per, hops_n), BF16),
            jax.ShapeDtypeStruct((devices_n * capacity, per, feat_n), BF16),
        ],
        compiler_params=pltpu.CompilerParams(
            vmem_limit_bytes=52 * 2**20,
            dimension_semantics=("arbitrary", "arbitrary"),
        ),
        cost_estimate=pl.CostEstimate(
            flops=flops, bytes_accessed=64 * 2**20, transcendentals=sensors * combos * per * hops_n
        ),
    )(
        orders.reshape(-1), owner_ids, places, first_channel.reshape(1),
        hops, coefficients, table, twist, gathered,
    )
    outgoing = outgoing.reshape(devices_n, capacity, per, feat_n)
    found = lax.all_to_all(outgoing, ("row", "col"), split_axis=0, concat_axis=0, tiled=True)
    return (spectrum, found[None])


def solution(mesh):
    in_specs = (P(None, "row", None), P(), P(("row", "col"), None), P(("row", "col"), None, None))
    out_specs = (
        P(None, None, None, ("row", "col"), None),
        P(("row", "col"), None, None, None, None),
    )
    return jax.shard_map(shards, mesh=mesh, in_specs=in_specs, out_specs=out_specs, check_vma=False)
```

profile of v0, /device:TPU:1, one launch (start us, length us, event | category | flops | bytes accessed | tf_op | source)
XLA Modules:
  0.0 375.3 jit_solution(10098279472012505635)
XLA Ops:
  7.2 0.0 copy-start
  7.2 0.0 copy-start.1
  7.2 0.0 all-gather.4.cloned.1.call-start
  7.2 0.7 all-gather.4.cloned.1.call-update
  7.9 0.0 all-gather.6.cloned.1.call-start
  8.0 0.8 copy-done
  8.8 1.0 copy.8
  9.8 0.0 all-gather.6.cloned.1.call-update
  9.8 0.8 reshape.42.orders_ref
  10.6 0.1 subtract_multiply_fusion
  10.6 0.1 fusion.20
  10.7 0.9 convert_reduce_fusion
  11.6 4.0 %fusion.12 = bf16[512,512]{1,0:T(8,128)(2,1)S(1)} fusion(), kind=kLoop, calls=%fused_computation.25 | loop fusion | flops 4718592 | bytes 524288 | tf_op jit(solution)/shard_map/neg | solution.py:34
  15.6 4.3 %sine_convert_fusion = (bf16[512,512]{1,0:T(8,128)(2,1)S(1)}, bf16[512,512]{1,0:T(8,128)(2,1)S(1)}) fusion(), kind=kLoop, calls=%fused_computation.14 | loop fusion | flops 4194304 | bytes 1048576 | tf_op jit(solution)/shard_map/convert_element_type | solution.py:32
  19.9 1.6 maximum_maximum_fusion.table_ref
  21.6 0.0 copy-done.1
  21.6 4.5 %multiply_convert_fusion.1 = (bf16[128,2048]{1,0:T(8,128)(2,1)S(1)}, bf16[128,2048]{1,0:T(8,128)(2,1)S(1)}) fusion(s32[128]{0:T(128)S(1)} %and_select_fusion, f32[2048]{0:T(1024)S(1)} %subtract_multiply_fusion), kind=kLoop, calls=%fused_computation.19 | loop fusion | flops 4718592 | bytes 1057280 | tf_op jit(solution)/shard_map/convert
  26.1 0.1 pad_maximum_fusion.coef_ref
  26.2 49.5 %all-gather.4.cloned.1.call-done.templates_ref = bf16[32,512,128]{2,1,0:T(8,128)(2,1)} async-done(((bf16[1,512,128]{2,1,0:T(8,128)(2,1)}), bf16[32,512,128]{2,1,0:T(8,128)(2,1)}) %all-gather.4.cloned.1.call-update) | async-done | bytes 4194320 | tf_op jit(solution)/shard_map/all_gather | solution.py:194
  75.7 117.0 %all-gather.6.cloned.1.call-done = bf16[128,8,16,512]{3,2,1,0:T(8,128)(2,1)} async-done(((bf16[4,8,16,512]{3,2,1,0:T(8,128)(2,1)}), bf16[128,8,16,512]{3,2,1,0:T(8,128)(2,1)}) %all-gather.6.cloned.1.call-update) | async-done | bytes 16777232 | tf_op jit(solution)/shard_map/all_gather | solution.py:191
  192.8 77.2 %shard_map.59 = (bf16[2,4,4,64,4096]{4,3,2,1,0:T(8,128)(2,1)}, bf16[256,64,128]{2,1,0:T(8,128)(2,1)}) custom-call(s32[4]{0:T(128)S(1)} %reshape.42.orders_ref, s32[128]{0:T(128)S(1)} %bitcast.11, s32[128]{0:T(128)S(1)} %multiply_add_fusion.places_ref, s32[1]{0:T(128)} %bitcast.1.first_ref, bf16[32,4,8,16,512]{4,3,2,1,0:T(8,128)(2,1)} %bitcast.14, ...), custom_call_target="tpu_custom_call" | custom-call | flops 34359738368 | bytes 67108864 | tf_op jit(solution)/shard_map/pallas_call | solution.py:214
  269.9 96.6 %all_to_all.5 = bf16[32,8,64,128]{3,2,1,0:T(8,128)(2,1)S(1)} all-to-all(bf16[32,8,64,128]{3,2,1,0:T(8,128)(2,1)} %bitcast.13), channel_id=1, replica_groups=mesh['row'=8,'col'=4] {'row','col'}, dimensions={0} | all-to-all | bytes 8388608 | tf_op jit(solution)/shard_map/all_to_all | solution.py:256
  366.5 2.0 copy.10
  (4 shorter events, 0.1 us)
Async XLA Ops:
  7.2 1.6 copy-start
  7.2 14.4 %copy-start.1 = (s32[128,1]{0,1:T(1,128)S(1)}, s32[128,1]{0,1:T(1,128)}, u32[]{:S(2)}) copy-start(s32[128,1]{0,1:T(1,128)} %param.6) | copy-start | bytes 1540
  7.2 68.5 %all-gather.4.cloned.1.call-start = ((), (), s32[]{:S(2)}) async-start(), calls=%async_computation.1 | async-start | bytes 4325376 | tf_op jit(solution)/shard_map/all_gather | solution.py:194
  7.9 184.8 %all-gather.6.cloned.1.call-start = ((), (), s32[]{:S(2)}) async-start(), calls=%async_computation.2 | async-start | bytes 17301504 | tf_op jit(solution)/shard_map/all_gather | solution.py:191
Sparse Core Ops, SparseCore 0:
  11.0 64.6 all-gather.3
  79.3 113.4 all-gather.5
where the time goes:
time: 376 us; the launch traced here: 375 us
  waiting for transfers between devices  167 us (44%)
  blocking collectives  96.6 us (26%)
  Pallas kernels  77.2 us (21%)
  other arithmetic  15.6 us (4%)
  between operations  14.1 us (4%)
  local copies, waits for them, and re-layouts  4.56 us (1%)
    all_gather x1, waiting for transfers between devices, shards(): hops = lax.all_gather(mine, ('row', 'col'), axis=0)  117 us
    all_to_all x1, blocking collectives, shards(): lax.all_to_all(outgoing, ('row', 'col'), split_axis=0, concat_axis=0, til...  96.6 us
    pallas_call x1, Pallas kernels, shards(): pl.pallas_call(functools.partial(spectra_kernel, combos=combos, per=per),...  77.2 us
    all_gather x1, waiting for transfers between devices, shards(): gathered = lax.all_gather(templates, ('row', 'col'), axis=0, tiled=True)  49.5 us
  transfers between devices with their start and end apart: 2, of which 2 were waited for; matrix products, arithmetic and copies ran while one was open for 5% of the time, Pallas kernels for 0%

commit v1 on v0

--- a/solution.py
+++ b/solution.py
@@ -82,10 +82,9 @@
 def spectra_kernel(
     orders_ref, owners_ref, places_ref, first_ref,
     frames_ref, coef_ref, table_ref, twist_ref, templates_ref,
-    spectrum_ref, outgoing_ref,
-    demod, product, section, feature,
-    *, combos, per,
+    *rest, combos, per, base,
 ):
+    spectrum_ref, outgoing_ref, demod, product, section, feature = rest[-6:]
     sensor, combo = pl.program_id(0), pl.program_id(1)
     sub = table_ref.shape[0] // 2
     frame = frames_ref.shape[-1]
@@ -93,7 +92,7 @@
 
     @pl.when((sensor == 0) & (combo == 0))
     def _():
-        outgoing_ref[...] = jnp.zeros_like(outgoing_ref)
+        outgoing_ref[...] = rest[1][...] if base else jnp.zeros_like(outgoing_ref)
 
     @pl.when(combo == 0)
     def _():
@@ -161,7 +160,7 @@
 
     lax.fori_loop(0, per // 16, rows_step, 0)
 
-    first_tile = (sensor * combos + combo) * RADIX
+    first_tile = ((base + sensor) * combos + combo) * RADIX
     for d in range(RADIX):
         owner = owners_ref[first_tile + d]
         place = places_ref[first_tile + d]
@@ -188,9 +187,13 @@
     mine = lax.dynamic_slice_in_dim(
         frames.reshape(sensors, hop_dev // RADIX, RADIX, frame_len), col_at * part, part, axis=1
     ).transpose(0, 2, 1, 3)
-    hops = lax.all_gather(mine, ("row", "col"), axis=0)
-    if part % 16:
-        hops = hops.transpose(1, 2, 0, 3, 4).reshape(1, sensors, RADIX, sub_n, frame_len)
+    half = sensors // 2
+    parts = []
+    for at in (0, half):
+        hops = lax.all_gather(mine[at : at + half], ("row", "col"), axis=0)
+        if part % 16:
+            hops = hops.transpose(1, 2, 0, 3, 4).reshape(1, half, RADIX, sub_n, frame_len)
+        parts.append(hops)
     gathered = lax.all_gather(templates, ("row", "col"), axis=0, tiled=True)
 
     first_channel = (row_at * cols_count + col_at) * per
@@ -209,49 +212,53 @@
     whole = lambda shape: pl.BlockSpec(
         shape, lambda s, c, *_: (0,) * len(shape), pipeline_mode=pl.Buffered(1)
     )
-    blocks = hops.shape[0]
-    flops = 2 * sensors * hops_n * channels_n * 4 * per + 2 * sensors * combos * RADIX * per * 4 * sub_n * sub_n
-    spectrum, outgoing = pl.pallas_call(
-        functools.partial(spectra_kernel, combos=combos, per=per),
-        grid_spec=pltpu.PrefetchScalarGridSpec(
-            num_scalar_prefetch=4,
-            grid=(sensors, combos),
-            in_specs=[
-                pl.BlockSpec(
-                    (blocks, 1, RADIX, hops.shape[3], frame_len),
-                    lambda s, c, *_: (0, s, 0, 0, 0),
-                ),
-                whole(coefficients.shape),
-                whole(table.shape),
-                whole(twist.shape),
-                whole(gathered.shape),
+    prior = ()
+    for base, hops in zip((0, half), parts):
+        blocks = hops.shape[0]
+        flops = 2 * half * hops_n * channels_n * 4 * per + 2 * half * combos * RADIX * per * 4 * sub_n * sub_n
+        prior = pl.pallas_call(
+            functools.partial(spectra_kernel, combos=combos, per=per, base=base),
+            grid_spec=pltpu.PrefetchScalarGridSpec(
+                num_scalar_prefetch=4,
+                grid=(half, combos),
+                in_specs=[
+                    pl.BlockSpec(
+                        (blocks, 1, RADIX, hops.shape[3], frame_len),
+                        lambda s, c, *_: (0, s, 0, 0, 0),
+                    ),
+                    whole(coefficients.shape),
+                    whole(table.shape),
+                    whole(twist.shape),
+                    whole(gathered.shape),
+                ] + ([pl.BlockSpec(memory_space=pl.ANY), whole(prior[1].shape)] if base else []),
+                out_specs=[
+                    pl.BlockSpec((2, 1, 1, per, hops_n), lambda s, c, *_: (0, base + s, c, 0, 0)),
+                    whole((devices_n * capacity, per, feat_n)),
+                ],
+                scratch_shapes=[
+                    pltpu.VMEM((2, RADIX, 2 * per, sub_n), BF16),
+                    pltpu.VMEM((combos, RADIX * per, 2 * sub_n), BF16),
+                    pltpu.VMEM((RADIX * per, 2 * sub_n), F32),
+                    pltpu.VMEM((RADIX, per, sub_n), BF16),
+                ],
+            ),
+            out_shape=[
+                jax.ShapeDtypeStruct((2, sensors, combos, per, hops_n), BF16),
+                jax.ShapeDtypeStruct((devices_n * capacity, per, feat_n), BF16),
             ],
-            out_specs=[
-                pl.BlockSpec((2, 1, 1, per, hops_n), lambda s, c, *_: (0, s, c, 0, 0)),
-                whole((devices_n * capacity, per, feat_n)),
-            ],
-            scratch_shapes=[
-                pltpu.VMEM((2, RADIX, 2 * per, sub_n), BF16),
-                pltpu.VMEM((combos, RADIX * per, 2 * sub_n), BF16),
-                pltpu.VMEM((RADIX * per, 2 * sub_n), F32),
-                pltpu.VMEM((RADIX, per, sub_n), BF16),
-            ],
-        ),
-        out_shape=[
-            jax.ShapeDtypeStruct((2, sensors, combos, per, hops_n), BF16),
-            jax.ShapeDtypeStruct((devices_n * capacity, per, feat_n), BF16),
-        ],
-        compiler_params=pltpu.CompilerParams(
-            vmem_limit_bytes=52 * 2**20,
-            dimension_semantics=("arbitrary", "arbitrary"),
-        ),
-        cost_estimate=pl.CostEstimate(
-            flops=flops, bytes_accessed=64 * 2**20, transcendentals=sensors * combos * per * hops_n
-        ),
-    )(
-        orders.reshape(-1), owner_ids, places, first_channel.reshape(1),
-        hops, coefficients, table, twist, gathered,
-    )
+            input_output_aliases={9: 0} if base else {},
+            compiler_params=pltpu.CompilerParams(
+                vmem_limit_bytes=52 * 2**20,
+                dimension_semantics=("arbitrary", "arbitrary"),
+            ),
+            cost_estimate=pl.CostEstimate(
+                flops=flops, bytes_accessed=32 * 2**20, transcendentals=half * combos * per * hops_n
+            ),
+        )(
+            orders.reshape(-1), owner_ids, places, first_channel.reshape(1),
+            hops, coefficients, table, twist, gathered, *prior,
+        )
+    spectrum, outgoing = prior
     outgoing = outgoing.reshape(devices_n, capacity, per, feat_n)
     found = lax.all_to_all(outgoing, ("row", "col"), split_axis=0, concat_axis=0, tiled=True)
     return (spectrum, found[None])

time: 376 us -> 383 us (1.019)
  Pallas kernels: 77.2 us -> 85.7 us
    pallas_call x1 -> x2, Pallas kernels: 77.2 us -> 85.7 us  [shards(): pl.pallas_call(functools.partial(spectra_kernel, combos=combos, per=per,...]
    all_gather x1 -> x2, waiting for transfers between devices: 117 us -> 116 us  [shards(): hops = lax.all_gather(mine[at:at + half], ('row', 'col'), axis=0)]
  transfers between devices with their start and end apart: 2 -> 3, of which waited for: 2 -> 3; matrix products, arithmetic and copies ran while one was open for 5% -> 5% of each run, Pallas kernels for 0% -> 11%
where the time goes in v1:
time: 383 us
  waiting for transfers between devices  166 us (43%)
  blocking collectives  97 us (25%)
  Pallas kernels  85.7 us (22%)
  other arithmetic  15.6 us (4%)
  between operations  13.8 us (4%)
  local copies, waits for them, and re-layouts  5.22 us (1%)
    all_gather x2, waiting for transfers between devices, shards(): hops = lax.all_gather(mine[at:at + half], ('row', 'col'), axis=0)  116 us
    all_to_all x1, blocking collectives, shards(): lax.all_to_all(outgoing, ('row', 'col'), split_axis=0, concat_axis=0, til...  97 us
    pallas_call x2, Pallas kernels, shards(): pl.pallas_call(functools.partial(spectra_kernel, combos=combos, per=per,...  85.7 us
    all_gather x1, waiting for transfers between devices, shards(): gathered = lax.all_gather(templates, ('row', 'col'), axis=0, tiled=True)  48.9 us
  transfers between devices with their start and end apart: 3, of which 3 were waited for; matrix products, arithmetic and copies ran while one was open for 5% of the time, Pallas kernels for 11%

profile of v1, /device:TPU:1, one launch (start us, length us, event | category | flops | bytes accessed | tf_op | source)
XLA Modules:
  0.0 383.0 jit_solution(3548845402238544142)
XLA Ops:
  7.2 0.0 copy-start
  7.2 0.0 all-gather.6.cloned.1.call-start
  7.2 0.7 all-gather.6.cloned.1.call-update
  7.9 0.0 all-gather.10.cloned.1.call-start
  8.0 0.8 copy-done
  8.8 0.0 copy-start.1
  8.9 0.8 copy.11
  9.6 0.0 all-gather.10.cloned.1.call-update
  9.7 0.0 all-gather.8.cloned.1.call-start
  9.7 0.8 copy.10
  10.5 0.0 all-gather.8.cloned.1.call-update
  10.5 0.8 reshape.44.orders_ref
  11.3 0.1 subtract_multiply_fusion
  11.4 0.1 fusion.20
  11.5 0.9 convert_reduce_fusion
  12.4 4.0 %fusion.12 = bf16[512,512]{1,0:T(8,128)(2,1)S(1)} fusion(), kind=kLoop, calls=%fused_computation.25 | loop fusion | flops 4718592 | bytes 524288 | tf_op jit(solution)/shard_map/neg | solution.py:34
  16.4 4.3 %sine_convert_fusion = (bf16[512,512]{1,0:T(8,128)(2,1)S(1)}, bf16[512,512]{1,0:T(8,128)(2,1)S(1)}) fusion(), kind=kLoop, calls=%fused_computation.14 | loop fusion | flops 4194304 | bytes 1048576 | tf_op jit(solution)/shard_map/convert_element_type | solution.py:32
  20.7 1.7 maximum_maximum_fusion.table_ref
  22.4 0.0 copy-done.1
  22.4 4.5 %multiply_convert_fusion.1 = (bf16[128,2048]{1,0:T(8,128)(2,1)S(1)}, bf16[128,2048]{1,0:T(8,128)(2,1)S(1)}) fusion(s32[128]{0:T(128)S(1)} %and_select_fusion, f32[2048]{0:T(1024)S(1)} %subtract_multiply_fusion), kind=kLoop, calls=%fused_computation.19 | loop fusion | flops 4718592 | bytes 1057280 | tf_op jit(solution)/shard_map/convert
  26.9 0.1 pad_maximum_fusion.coef_ref
  27.0 48.9 %all-gather.6.cloned.1.call-done.templates_ref = bf16[32,512,128]{2,1,0:T(8,128)(2,1)} async-done(((bf16[1,512,128]{2,1,0:T(8,128)(2,1)}), bf16[32,512,128]{2,1,0:T(8,128)(2,1)}) %all-gather.6.cloned.1.call-update) | async-done | bytes 4194320 | tf_op jit(solution)/shard_map/all_gather | solution.py:197
  75.8 79.5 %all-gather.10.cloned.1.call-done = bf16[64,8,16,512]{3,2,1,0:T(8,128)(2,1)} async-done(((bf16[2,8,16,512]{3,2,1,0:T(8,128)(2,1)}), bf16[64,8,16,512]{3,2,1,0:T(8,128)(2,1)}) %all-gather.10.cloned.1.call-update) | async-done | bytes 8388624 | tf_op jit(solution)/shard_map/all_gather | solution.py:193
  155.3 42.3 %shard_map.59 = (bf16[2,4,4,64,4096]{4,3,2,1,0:T(8,128)(2,1)}, bf16[256,64,128]{2,1,0:T(8,128)(2,1)}) custom-call(s32[4]{0:T(128)S(1)} %reshape.44.orders_ref, s32[128]{0:T(128)S(1)} %bitcast.12, s32[128]{0:T(128)S(1)} %multiply_add_fusion.places_ref, s32[1]{0:T(128)} %bitcast.1.first_ref, bf16[32,2,8,16,512]{4,3,2,1,0:T(8,128)(2,1)} %bitcast.16, ...), custom_call_target="tpu_custom_call" | custom-call | flops 17179869184 | bytes 33554432 | tf_op jit(solution)/shard_map/pallas_call | solution.py:219
  197.6 36.5 %all-gather.8.cloned.1.call-done = bf16[64,8,16,512]{3,2,1,0:T(8,128)(2,1)} async-done(((bf16[2,8,16,512]{3,2,1,0:T(8,128)(2,1)}), bf16[64,8,16,512]{3,2,1,0:T(8,128)(2,1)}) %all-gather.8.cloned.1.call-update) | async-done | bytes 8388624 | tf_op jit(solution)/shard_map/all_gather | solution.py:193
  234.1 43.4 %shard_map.60 = (bf16[2,4,4,64,4096]{4,3,2,1,0:T(8,128)(2,1)}, bf16[256,64,128]{2,1,0:T(8,128)(2,1)}) custom-call(s32[4]{0:T(128)S(1)} %reshape.44.orders_ref, s32[128]{0:T(128)S(1)} %bitcast.13, s32[128]{0:T(128)S(1)} %multiply_add_fusion.places_ref, s32[1]{0:T(128)} %bitcast.1.first_ref, ...), custom_call_target="tpu_custom_call", output_to_operand_aliasing={{0}: (9, {})} | custom-call | flops 17179869184 | bytes 33554432 | tf_op jit(solution)/shard_map/pallas_call | solution.py:219
  277.5 97.0 %all_to_all.5 = bf16[32,8,64,128]{3,2,1,0:T(8,128)(2,1)S(1)} all-to-all(bf16[32,8,64,128]{3,2,1,0:T(8,128)(2,1)} %bitcast.15), channel_id=1, replica_groups=mesh['row'=8,'col'=4] {'row','col'}, dimensions={0} | all-to-all | bytes 8388608 | tf_op jit(solution)/shard_map/all_to_all | solution.py:263
  374.5 2.0 copy.14
  (5 shorter events, 0.1 us)
Async XLA Ops:
  7.2 1.6 copy-start
  7.2 68.6 %all-gather.6.cloned.1.call-start = ((), (), s32[]{:S(2)}) async-start(), calls=%async_computation.1 | async-start | bytes 4325376 | tf_op jit(solution)/shard_map/all_gather | solution.py:197
  7.9 147.4 %all-gather.10.cloned.1.call-start = ((), (), s32[]{:S(2)}) async-start(), calls=%async_computation.3 | async-start | bytes 8650752 | tf_op jit(solution)/shard_map/all_gather | solution.py:193
  8.8 13.6 %copy-start.1 = (s32[128,1]{0,1:T(1,128)S(1)}, s32[128,1]{0,1:T(1,128)}, u32[]{:S(2)}) copy-start(s32[128,1]{0,1:T(1,128)} %param.6) | copy-start | bytes 1540
  9.7 224.4 %all-gather.8.cloned.1.call-start = ((), (), s32[]{:S(2)}) async-start(), calls=%async_computation.2 | async-start | bytes 8650752 | tf_op jit(solution)/shard_map/all_gather | solution.py:193
Sparse Core Ops, SparseCore 0:
  11.0 64.7 all-gather.5
  79.3 75.9 all-gather.9
  158.2 75.8 all-gather.7
